TPU v7x, 256 devices: a whole 4x4x8 slice. The times are simulated.
256 devices in a mesh: grp: 16 (over z, core), sp: 16 (over y, x).
Axes of the slice: x: 4, y: 4, z: 8, core: 2. Of those that a mesh axis runs over, the one named last changes fastest.
Arguments:
- queries: bfloat16 [32768, 2048], P(('grp', 'sp')), may hold values from -9 to 9
- keys: bfloat16 [32768, 512], P(('grp', 'sp')), may hold values from -9 to 9
- values: bfloat16 [32768, 512], P(('grp', 'sp')), may hold values from -6 to 6
- grad_out: bfloat16 [32768, 2048], P(('grp', 'sp')), may hold values from -6 to 6
- doc_ids: int32 [32768], P(('grp', 'sp')), may hold values from 0 to 63, never falling along the last dimension, each value on 1 to 2048 neighbouring positions
Outputs:
- grad_queries: bfloat16 [32768, 2048], P(('grp', 'sp'))
- grad_keys: bfloat16 [32768, 512], P(('grp', 'sp'))
- grad_values: bfloat16 [32768, 512], P(('grp', 'sp'))
Inputs may be any that keep to these rules, and one draw needn't show every extreme that they name: `doc_ids`: document numbers never fall along the stream; every document has 1 to 2048 tokens and one has exactly 2048.
All inputs are finite; a program needn't handle non-finite values.
Results may differ from a plain program's by a relative error of at most 0.0066.
Values may be sent and summed in bfloat16 or wider, within the bound.
A program may use at most 128 MiB of HBM per device.

v0:
```python
import functools
import math

import jax
import jax.numpy as jnp
from jax import lax
from jax.experimental import pallas as pl
from jax.experimental.pallas import tpu as pltpu
from jax.sharding import PartitionSpec as P

HEADS = 16
KV_HEADS = 4
HEAD_DIM = 128
RATIO = HEADS // KV_HEADS
SIDE = 4
TOK = 128
QUARTER = SIDE * TOK
BACK = 4
KEYS = (BACK + 1) * QUARTER
TILE = 256
TILES = KEYS // TILE
SCALE = 1.0 / math.sqrt(HEAD_DIM)
EXP2_SCALE = SCALE * math.log2(math.e)
MASKED = -1e30
ORDER = (3, 2, 1, 4, 0)
MESH = pl.DeviceIdType.MESH
F32 = jnp.float32
BF16 = jnp.bfloat16


def tile_rows(tile):
    if tile == 0:
        return 0, TILE
    if tile == TILES - 1:
        return QUARTER - TILE, TILE
    return 0, QUARTER


def kernel(
    groups,
    q_ref, g_ref, k_ref, v_ref, id_ref,
    dq_ref, dk_ref, dv_ref,
    q_all, g_all, kv_all, id_all, kt_all, idk_all,
    e_all, dp_all, m_all, l_all, ed_all, delta_all,
    dqt, dk_sum, dv_sum, dq_out, dkv_out, dkv_in, dkv_last,
    loc_sem, sent, side_in, along_in, back_in,
):
    grp = lax.axis_index("grp")
    sp = lax.axis_index("sp")
    y = sp // SIDE
    x = lax.rem(sp, SIDE)
    total = groups * SIDE
    quarter = grp * SIDE + y

    def side(o):
        other = lax.rem(x + o, SIDE)
        return {"sp": y * SIDE + other}, other

    def along(o):
        other = lax.rem(quarter + o + total, total)
        return {"grp": other // SIDE, "sp": lax.rem(other, SIDE) * SIDE + x}

    def plane(o):
        return {"sp": lax.rem(y + o, SIDE) * SIDE + x}

    def next_group(o):
        return {"grp": lax.rem(grp + o, groups)}

    barrier = pltpu.get_barrier_semaphore()
    for o in range(1, SIDE):
        pl.semaphore_signal(barrier, inc=1, device_id=side(o)[0], device_id_type=MESH)
        pl.semaphore_signal(barrier, inc=1, device_id=plane(o), device_id_type=MESH)
    for o in (1, groups - 1):
        pl.semaphore_signal(barrier, inc=1, device_id=next_group(o), device_id_type=MESH)

    own = BACK * QUARTER
    my_rows = pl.ds(pl.multiple_of(x * TOK, TOK), TOK)
    my_keys = pl.ds(pl.multiple_of(own + x * TOK, TOK), TOK)

    def columns(head):
        return pl.ds(pl.multiple_of(head * HEAD_DIM, HEAD_DIM), HEAD_DIM)

    def remote(src, dst, send, recv, device):
        return pltpu.make_async_remote_copy(
            src_ref=src, dst_ref=dst, send_sem=send, recv_sem=recv, device_id=device, device_id_type=MESH
        )

    def kv_side(i, o):
        device, other = side(o)
        source = (k_ref, v_ref)[i]
        return remote(source.at[:, columns(other)], kv_all.at[i, my_keys], sent.at[i], side_in.at[i * SIDE + o], device)

    def id_side(o):
        device, _ = side(o)
        return remote(id_ref, id_all.at[BACK * SIDE + x], sent.at[2], side_in.at[0], device)

    def qg_side(i, h, o):
        device, other = side(o)
        source, target = ((q_ref, q_all), (g_ref, g_all))[i]
        at = 2 * SIDE + i * RATIO + h
        cols = columns(other * RATIO + h)
        return remote(source.at[:, cols], target.at[h, my_rows], sent.at[3 + i], side_in.at[at], device)

    def kv_local(i):
        source = (k_ref, v_ref)[i]
        return pltpu.make_async_copy(source.at[:, columns(x)], kv_all.at[i, my_keys], loc_sem.at[i])

    def id_local():
        return pltpu.make_async_copy(id_ref, id_all.at[BACK * SIDE + x], loc_sem.at[2])

    def qg_local(i, h):
        source, target = ((q_ref, q_all), (g_ref, g_all))[i]
        return pltpu.make_async_copy(
            source.at[:, columns(x * RATIO + h)], target.at[h, my_rows], loc_sem.at[3 + i * RATIO + h]
        )

    def keys_of(back):
        return pl.ds((BACK - back) * QUARTER, QUARTER)

    def kv_along(i, back, o, source=0):
        device = next_group(1) if back == BACK else plane(back)
        first = lax.rem(x + SIDE - o, SIDE) * TOK
        src = pl.ds(pl.multiple_of((BACK - source) * QUARTER + first, TOK), TOK)
        dst = pl.ds(pl.multiple_of((BACK - back) * QUARTER + first, TOK), TOK)
        at = i * 2 * SIDE + (o if back == BACK else SIDE + back)
        return remote(kv_all.at[i, src], kv_all.at[i, dst], sent.at[5 + i], along_in.at[at], device)

    def id_along(back, source=0):
        device = next_group(1) if back == BACK else plane(back)
        src = pl.ds((BACK - source) * SIDE, SIDE)
        dst = pl.ds((BACK - back) * SIDE, SIDE)
        return remote(id_all.at[src], id_all.at[dst], sent.at[7], along_in.at[4 * SIDE + back - 1], device)

    def dkv_along(i, back):
        at = back - 1
        return remote(dkv_out.at[at, i], dkv_in.at[at, i], sent.at[8 + i], back_in.at[i], along(-back))

    def dq_side(h, o):
        device, other = side(o)
        rows = pl.ds(pl.multiple_of(other * TOK, TOK), TOK)
        return remote(
            dq_out.at[h, rows], dq_ref.at[:, columns(x * RATIO + h)], sent.at[10], back_in.at[2], device
        )

    def dq_local(h):
        return pltpu.make_async_copy(dq_out.at[h, my_rows], dq_ref.at[:, columns(x * RATIO + h)], loc_sem.at[11 + h])

    def dkv_side(i, o):
        device, other = side(o)
        rows = pl.ds(pl.multiple_of(other * TOK, TOK), TOK)
        out = (dk_ref, dv_ref)[i]
        return remote(dkv_last.at[i, rows], out.at[:, columns(x)], sent.at[11 + i], back_in.at[3 + i], device)

    def dkv_local(i):
        out = (dk_ref, dv_ref)[i]
        return pltpu.make_async_copy(dkv_last.at[i, my_rows], out.at[:, columns(x)], loc_sem.at[15 + i])

    def later(start):
        for back in range(1, BACK):

            @pl.when(y + back < SIDE)
            def _(back=back):
                start(back)

    def earlier(start):
        for back in range(1, BACK):

            @pl.when(y + back >= SIDE)
            def _(back=back):
                start(back)

    def start_qg(i):
        for h in range(RATIO):
            for o in range(1, SIDE):
                qg_side(i, h, o).start()

    chunks = (0, 1, 3, 2)

    def wait_chunk(i, o):
        if o == 0:
            kv_local(i).wait()
        else:
            kv_side(i, o).wait_recv()

    def arrived(ref, sem):
        pltpu.make_async_copy(ref, ref, sem).wait()

    three = pl.ds(0, (SIDE - 1) * TOK)

    kv_local(0).start()
    id_local().start()
    kv_local(1).start()
    for i in range(2):
        for h in range(RATIO):
            qg_local(i, h).start()
    pl.semaphore_wait(barrier, 2 * SIDE)
    for o in range(1, SIDE):
        kv_side(0, o).start()
    for o in range(1, SIDE):
        id_side(o).start()
    for o in range(1, SIDE):
        kv_side(1, o).start()

    for o in chunks:
        wait_chunk(0, o)
        kv_along(0, BACK, o).start()
        later(lambda back, o=o: kv_along(0, back, o).start())
        if o == 0:
            start_qg(0)
    id_local().wait()
    arrived(id_all.at[pl.ds(0, SIDE - 1)], side_in.at[0])
    id_along(BACK).start()
    later(lambda back: id_along(back).start())
    for o in chunks:
        wait_chunk(1, o)
        kv_along(1, BACK, o).start()
    start_qg(1)

    row_at = lax.broadcasted_iota(jnp.int32, (TOK, TOK), 0)
    col_at = lax.broadcasted_iota(jnp.int32, (TOK, TOK), 1)
    ones = jnp.ones((TOK, TOK), BF16)

    def spread_ids(back):
        first = (BACK - back) * SIDE
        for i in range(SIDE):
            ids = jnp.broadcast_to(id_all[first + i].astype(F32), (TOK, TOK))
            diagonal = jnp.where(row_at == col_at, ids, 0.0).astype(BF16)
            idk_all[pl.ds((first + i) * TOK, TOK), :] = jnp.dot(diagonal, ones, preferred_element_type=F32)
        keys = kv_all[0, keys_of(back), :]
        kt_all[:, keys_of(back)] = keys.astype(F32).T.astype(BF16)

    def first_pass(h, tile):
        row, count = tile_rows(tile)
        keys = pl.ds(tile * TILE, TILE)
        rows = pl.ds(row, count)
        across = (((1,), (1,)), ((), ()))
        scores = lax.dot_general(kv_all[0, keys, :], q_all[h, rows, :], across, preferred_element_type=F32)
        idk = idk_all[keys, :]
        parts = []
        for c in range(count // TOK):
            allowed = idk == id_all[BACK * SIDE + row // TOK + c].astype(F32)
            key_first = tile * TILE - own
            row_first = row + c * TOK
            if key_first + TILE - 1 > row_first:
                key_pos = key_first + lax.broadcasted_iota(jnp.int32, (TILE, TOK), 0)
                row_pos = row_first + lax.broadcasted_iota(jnp.int32, (TILE, TOK), 1)
                allowed = allowed & (key_pos <= row_pos)
            parts.append(jnp.where(allowed, scores[:, c * TOK : (c + 1) * TOK] * EXP2_SCALE, MASKED))
        scores = jnp.concatenate(parts, axis=1)
        top = jnp.max(scores, axis=0, keepdims=True)
        terms = jnp.exp2(scores - top)
        e_all[h, tile, :, rows] = terms
        m_all[h, tile, :, rows] = top
        l_all[h, tile, :, rows] = jnp.sum(terms, axis=0, keepdims=True)

    for o in chunks:
        kv_along(0, BACK, o).wait_recv()
        earlier(lambda back, o=o: kv_along(0, back, o, BACK).start())
        if o == 0:
            for one in chunks:
                later(lambda back, one=one: kv_along(1, back, one).start())
    id_along(BACK).wait_recv()
    earlier(lambda back: id_along(back, BACK).start())

    def tiles_of(back):
        return (2 * (BACK - back), 2 * (BACK - back) + 1)

    spread_ids(0)
    spread_ids(BACK)
    for back in (0, 4, 1, 3, 2):
        if 0 < back < BACK:
            arrived(kv_all.at[0, keys_of(back)], along_in.at[SIDE + back])
            id_along(back).wait_recv()
            spread_ids(back)

        @pl.loop(0, RATIO, unroll=True)
        def _(h, back=back):
            if back == 0:
                qg_local(0, h).wait()
                arrived(q_all.at[h, three], side_in.at[2 * SIDE + h])
            for tile in tiles_of(back):
                first_pass(h, tile)

        if back == BACK:
            for o in chunks:
                kv_along(1, BACK, o).wait_recv()
                earlier(lambda back, o=o: kv_along(1, back, o, BACK).start())

    halves = range(QUARTER // TILE)

    def tiles_for(half):
        return [t for t in range(TILES) if not (t == 0 and half == 1) and not (t == TILES - 1 and half == 0)]

    @pl.loop(0, RATIO, unroll=True)
    def _(h):
        for half in halves:
            rows = pl.ds(half * TILE, TILE)
            tiles = tiles_for(half)
            tops = [m_all[h, t, :, rows] for t in tiles]
            top = functools.reduce(jnp.maximum, tops)
            weights = [jnp.exp2(one - top) for one in tops]
            inverse = 1.0 / sum(w * l_all[h, t, :, rows] for w, t in zip(weights, tiles))
            for w, t in zip(weights, tiles):
                m_all[h, t, :, rows] = w * inverse
        dqt[h] = jnp.zeros((HEAD_DIM, QUARTER), F32)

    def value_pass(h, tile):
        row, count = tile_rows(tile)
        rows = pl.ds(row, count)
        low = (e_all[h, tile, :, rows] * m_all[h, tile, :, rows]).astype(BF16)
        at = pl.ds((tile % 2) * TILE, TILE)
        dv_sum[at, :] += jnp.dot(low, g_all[h, rows, :], preferred_element_type=F32)

    for h in range(RATIO):
        qg_local(1, h).wait()
        arrived(g_all.at[h, three], side_in.at[2 * SIDE + RATIO + h])
    for back in ORDER:
        dv_sum[...] = jnp.zeros_like(dv_sum)

        @pl.loop(0, RATIO, unroll=True)
        def _(h, back=back):
            for tile in tiles_of(back):
                value_pass(h, tile)

        if back > 0:
            dkv_out[back - 1, 1] = dv_sum[...].astype(BF16)
            dkv_along(1, back).start()

    def delta_pass(h, tile):
        row, count = tile_rows(tile)
        keys = pl.ds(tile * TILE, TILE)
        rows = pl.ds(row, count)
        across = (((1,), (1,)), ((), ()))
        dp = lax.dot_general(kv_all[1, keys, :], g_all[h, rows, :], across, preferred_element_type=F32)
        dp_all[h, tile, :, rows] = dp
        ed_all[h, tile, :, rows] = jnp.sum(e_all[h, tile, :, rows] * dp, axis=0, keepdims=True)

    for back in (0, 4, 1, 3, 2):
        if 0 < back < BACK:
            arrived(kv_all.at[1, keys_of(back)], along_in.at[2 * SIDE + SIDE + back])

        @pl.loop(0, RATIO, unroll=True)
        def _(h, back=back):
            for tile in tiles_of(back):
                delta_pass(h, tile)

    @pl.loop(0, RATIO, unroll=True)
    def _(h):
        for half in halves:
            rows = pl.ds(half * TILE, TILE)
            delta_all[h, :, rows] = sum(m_all[h, t, :, rows] * ed_all[h, t, :, rows] for t in tiles_for(half))

    def key_pass(h, tile):
        row, count = tile_rows(tile)
        keys = pl.ds(tile * TILE, TILE)
        rows = pl.ds(row, count)
        probs = e_all[h, tile, :, rows] * m_all[h, tile, :, rows]
        ds = (probs * (dp_all[h, tile, :, rows] - delta_all[h, :, rows])).astype(BF16)
        dqt[h, :, rows] += jnp.dot(kt_all[:, keys], ds, preferred_element_type=F32)
        at = pl.ds((tile % 2) * TILE, TILE)
        dk_sum[at, :] += jnp.dot(ds, q_all[h, rows, :], preferred_element_type=F32)

    for back in ORDER:
        dk_sum[...] = jnp.zeros_like(dk_sum)

        @pl.loop(0, RATIO, unroll=True)
        def _(h, back=back):
            for tile in tiles_of(back):
                key_pass(h, tile)
            if back == 0:
                dq_out[h] = (dqt[h] * SCALE).T.astype(BF16)
                for o in range(1, SIDE):
                    dq_side(h, o).start()
                dq_local(h).start()

        if back > 0:
            dkv_out[back - 1, 0] = (dk_sum[...] * SCALE).astype(BF16)
            dkv_along(0, back).start()

    arrived(id_all.at[pl.ds(0, SIDE - 1)], sent.at[2])
    arrived(id_all.at[pl.ds(0, SIDE * SIDE)], sent.at[7])
    for i in range(2):
        arrived(kv_all.at[i, three], sent.at[i])
        arrived(q_all.at[pl.ds(0, SIDE - 1)], sent.at[3 + i])
        arrived(q_all, sent.at[5 + i])

    for i in (1, 0):
        one = dk_sum[...] * SCALE if i == 0 else dv_sum[...]
        arrived(q_all, back_in.at[i])
        for back in range(1, BACK + 1):
            one = one + dkv_in[back - 1, i].astype(F32)
        dkv_last[i] = one.astype(BF16)
        for o in range(1, SIDE):
            dkv_side(i, o).start()
        dkv_local(i).start()

    arrived(q_all, sent.at[8])
    arrived(q_all, sent.at[9])
    for h in range(RATIO):
        dq_local(h).wait()
    arrived(q_all.at[pl.ds(0, SIDE - 1)], sent.at[10])
    arrived(q_all.at[pl.ds(0, SIDE - 1)], back_in.at[2])
    for i in (1, 0):
        dkv_local(i).wait()
        arrived(dkv_last.at[i, three], sent.at[11 + i])
        arrived(dkv_last.at[i, three], back_in.at[3 + i])


def copy_kernel(*refs):
    count = (len(refs) - 2) // 3
    slabs = []
    for source, target, held in zip(refs[:count], refs[count : 2 * count], refs[2 * count : 3 * count]):
        for first in range(0, source.shape[1], 4 * HEAD_DIM):
            cols = pl.ds(first, 4 * HEAD_DIM)
            slabs.append((source.at[:, cols], held.at[:, cols], target.at[:, cols]))
    read, write = refs[-2:]
    ins = [pltpu.make_async_copy(a, b, read.at[n]) for n, (a, b, _) in enumerate(slabs)]
    outs = [pltpu.make_async_copy(b, c, write.at[n]) for n, (_, b, c) in enumerate(slabs)]
    for copy in ins:
        copy.start()
    for one, two in zip(ins, outs):
        one.wait()
        two.start()
    for copy in outs:
        copy.wait()


def copied(arrays):
    count = len(arrays)
    slabs = sum(a.shape[1] // (4 * HEAD_DIM) for a in arrays)
    return pl.pallas_call(
        copy_kernel,
        out_shape=tuple(jax.ShapeDtypeStruct(a.shape, a.dtype) for a in arrays),
        in_specs=[pl.BlockSpec(memory_space=pl.ANY)] * count,
        out_specs=[pl.BlockSpec(memory_space=pl.ANY)] * count,
        scratch_shapes=[pltpu.VMEM(a.shape, a.dtype) for a in arrays]
        + [pltpu.SemaphoreType.DMA((slabs,)), pltpu.SemaphoreType.DMA((slabs,))],
    )(*arrays)


def body(groups, queries, keys, values, grad_out, doc_ids):
    dma = pltpu.SemaphoreType.DMA
    outs = pl.pallas_call(
        functools.partial(kernel, groups),
        out_shape=(
            jax.ShapeDtypeStruct((TOK, HEADS * HEAD_DIM), BF16),
            jax.ShapeDtypeStruct((TOK, KV_HEADS * HEAD_DIM), BF16),
            jax.ShapeDtypeStruct((TOK, KV_HEADS * HEAD_DIM), BF16),
        ),
        in_specs=[pl.BlockSpec(memory_space=pl.ANY)] * 5,
        out_specs=[pl.BlockSpec(memory_space=pl.ANY)] * 3,
        scratch_shapes=[
            pltpu.VMEM((RATIO, QUARTER, HEAD_DIM), BF16),
            pltpu.VMEM((RATIO, QUARTER, HEAD_DIM), BF16),
            pltpu.VMEM((2, KEYS, HEAD_DIM), BF16),
            pltpu.VMEM(((BACK + 1) * SIDE, 1, TOK), jnp.int32),
            pltpu.VMEM((HEAD_DIM, KEYS), BF16),
            pltpu.VMEM((KEYS, TOK), F32),
            pltpu.VMEM((RATIO, TILES, TILE, QUARTER), F32),
            pltpu.VMEM((RATIO, TILES, TILE, QUARTER), F32),
            pltpu.VMEM((RATIO, TILES, 1, QUARTER), F32),
            pltpu.VMEM((RATIO, TILES, 1, QUARTER), F32),
            pltpu.VMEM((RATIO, TILES, 1, QUARTER), F32),
            pltpu.VMEM((RATIO, 1, QUARTER), F32),
            pltpu.VMEM((RATIO, HEAD_DIM, QUARTER), F32),
            pltpu.VMEM((QUARTER, HEAD_DIM), F32),
            pltpu.VMEM((QUARTER, HEAD_DIM), F32),
            pltpu.VMEM((RATIO, QUARTER, HEAD_DIM), BF16),
            pltpu.VMEM((BACK, 2, QUARTER, HEAD_DIM), BF16),
            pltpu.VMEM((BACK, 2, QUARTER, HEAD_DIM), BF16),
            pltpu.VMEM((2, QUARTER, HEAD_DIM), BF16),
            dma((17,)),
            dma((13,)),
            dma((4 * SIDE,)),
            dma((5 * SIDE,)),
            dma((5,)),
        ],
        compiler_params=pltpu.CompilerParams(
            collective_id=0, has_side_effects=True, vmem_limit_bytes=60 * 1024 * 1024
        ),
    )(queries, grad_out, keys, values, doc_ids.reshape(1, TOK))
    return copied(outs)


def solution(mesh):
    return jax.shard_map(
        functools.partial(body, mesh.shape["grp"]),
        mesh=mesh,
        in_specs=(
            P(("grp", "sp"), None),
            P(("grp", "sp"), None),
            P(("grp", "sp"), None),
            P(("grp", "sp"), None),
            P(("grp", "sp")),
        ),
        out_specs=(P(("grp", "sp"), None), P(("grp", "sp"), None), P(("grp", "sp"), None)),
        check_vma=False,
    )
```

profile of v0, /device:TPU:4, one launch (start us, length us, event | category | flops | bytes accessed | tf_op | source)
XLA Modules:
  0.0 49.3 jit_solution(12534959623541332032)
XLA Ops:
  0.6 46.6 %shard_map.76 = (bf16[128,2048]{1,0:T(8,128)(2,1)}, bf16[128,512]{1,0:T(8,128)(2,1)}, bf16[128,512]{1,0:T(8,128)(2,1)}) custom-call(bf16[128,2048]{1,0:T(8,128)(2,1)} %q_ref.1, bf16[128,2048]{1,0:T(8,128)(2,1)} %g_ref.1, bf16[128,512]{1,0:T(8,128)(2,1)} %k_ref.1, bf16[128,512]{1,0:T(8,128)(2,1)} %v_ref.1, s32[1,128]{1,0:T(1,128)} %bitcast.1), custom_call_target="tpu_custom_call" | custom-call | tf_op jit(solution)/shard_map/pallas_call | solution.py:443
  47.2 2.0 %shard_map.77 = (bf16[128,2048]{1,0:T(8,128)(2,1)}, bf16[128,512]{1,0:T(8,128)(2,1)}, bf16[128,512]{1,0:T(8,128)(2,1)}) custom-call(bf16[128,2048]{1,0:T(8,128)(2,1)} %get-tuple-element.6.refs_0_, bf16[128,512]{1,0:T(8,128)(2,1)} %get-tuple-element.7.refs_1_, bf16[128,512]{1,0:T(8,128)(2,1)} %get-tuple-element.8.refs_2_), custom_call_target="tpu_custom_call" | custom-call | tf_op jit(solution)/shard_map/pallas_call | solution.py:431
where the time goes:
time: 49.4 us; the launch traced here: 49.3 us
  Pallas kernels  48.5 us (98%)
  between operations  0.8 us (2%)
    pallas_call x1, Pallas kernels, body(): pl.pallas_call(functools.partial(kernel, groups), out_shape=(jax.ShapeDty...  46.6 us
    pallas_call x1, Pallas kernels, copied(): pl.pallas_call(copy_kernel, out_shape=tuple((jax.ShapeDtypeStruct(a.shape...  1.97 us

commit v1 on v0

--- a/solution.py
+++ b/solution.py
@@ -42,7 +42,7 @@
     dq_ref, dk_ref, dv_ref,
     q_all, g_all, kv_all, id_all, kt_all, idk_all,
     e_all, dp_all, m_all, l_all, ed_all, delta_all,
-    dqt, dk_sum, dv_sum, dq_out, dkv_out, dkv_in, dkv_last,
+    dk_sum, dv_sum, dq_out, dkv_out, dkv_in, dkv_last,
     loc_sem, sent, side_in, along_in, back_in,
 ):
     grp = lax.axis_index("grp")
@@ -214,6 +214,7 @@
     for o in chunks:
         wait_chunk(1, o)
         kv_along(1, BACK, o).start()
+        later(lambda back, o=o: kv_along(1, back, o).start())
     start_qg(1)
 
     row_at = lax.broadcasted_iota(jnp.int32, (TOK, TOK), 0)
@@ -256,9 +257,6 @@
     for o in chunks:
         kv_along(0, BACK, o).wait_recv()
         earlier(lambda back, o=o: kv_along(0, back, o, BACK).start())
-        if o == 0:
-            for one in chunks:
-                later(lambda back, one=one: kv_along(1, back, one).start())
     id_along(BACK).wait_recv()
     earlier(lambda back: id_along(back, BACK).start())
 
@@ -302,7 +300,6 @@
             inverse = 1.0 / sum(w * l_all[h, t, :, rows] for w, t in zip(weights, tiles))
             for w, t in zip(weights, tiles):
                 m_all[h, t, :, rows] = w * inverse
-        dqt[h] = jnp.zeros((HEAD_DIM, QUARTER), F32)
 
     def value_pass(h, tile):
         row, count = tile_rows(tile)
@@ -355,10 +352,22 @@
         keys = pl.ds(tile * TILE, TILE)
         rows = pl.ds(row, count)
         probs = e_all[h, tile, :, rows] * m_all[h, tile, :, rows]
-        ds = (probs * (dp_all[h, tile, :, rows] - delta_all[h, :, rows])).astype(BF16)
-        dqt[h, :, rows] += jnp.dot(kt_all[:, keys], ds, preferred_element_type=F32)
+        ds = probs * (dp_all[h, tile, :, rows] - delta_all[h, :, rows])
+        dp_all[h, tile, :, rows] = ds
         at = pl.ds((tile % 2) * TILE, TILE)
-        dk_sum[at, :] += jnp.dot(ds, q_all[h, rows, :], preferred_element_type=F32)
+        dk_sum[at, :] += jnp.dot(ds.astype(BF16), q_all[h, rows, :], preferred_element_type=F32)
+
+    def query_grad(h):
+        for half in halves:
+            rows = pl.ds(half * TILE, TILE)
+            first = half * TILE
+            ds = [dp_all[h, t, :, rows].astype(BF16) for t in tiles_for(half)]
+            keys = kt_all[:, first : first + len(ds) * TILE]
+            dqt = jnp.dot(keys, jnp.concatenate(ds, axis=0), preferred_element_type=F32)
+            dq_out[h, rows, :] = (dqt * SCALE).T.astype(BF16)
+        for o in range(1, SIDE):
+            dq_side(h, o).start()
+        dq_local(h).start()
 
     for back in ORDER:
         dk_sum[...] = jnp.zeros_like(dk_sum)
@@ -367,15 +376,13 @@
         def _(h, back=back):
             for tile in tiles_of(back):
                 key_pass(h, tile)
-            if back == 0:
-                dq_out[h] = (dqt[h] * SCALE).T.astype(BF16)
-                for o in range(1, SIDE):
-                    dq_side(h, o).start()
-                dq_local(h).start()
 
         if back > 0:
             dkv_out[back - 1, 0] = (dk_sum[...] * SCALE).astype(BF16)
             dkv_along(0, back).start()
+
+    for h in range(RATIO):
+        query_grad(h)
 
     arrived(id_all.at[pl.ds(0, SIDE - 1)], sent.at[2])
     arrived(id_all.at[pl.ds(0, SIDE * SIDE)], sent.at[7])
@@ -410,8 +417,8 @@
     count = (len(refs) - 2) // 3
     slabs = []
     for source, target, held in zip(refs[:count], refs[count : 2 * count], refs[2 * count : 3 * count]):
-        for first in range(0, source.shape[1], 4 * HEAD_DIM):
-            cols = pl.ds(first, 4 * HEAD_DIM)
+        for first in range(0, source.shape[1], 2 * HEAD_DIM):
+            cols = pl.ds(first, 2 * HEAD_DIM)
             slabs.append((source.at[:, cols], held.at[:, cols], target.at[:, cols]))
     read, write = refs[-2:]
     ins = [pltpu.make_async_copy(a, b, read.at[n]) for n, (a, b, _) in enumerate(slabs)]
@@ -427,7 +434,7 @@
 
 def copied(arrays):
     count = len(arrays)
-    slabs = sum(a.shape[1] // (4 * HEAD_DIM) for a in arrays)
+    slabs = sum(a.shape[1] // (2 * HEAD_DIM) for a in arrays)
     return pl.pallas_call(
         copy_kernel,
         out_shape=tuple(jax.ShapeDtypeStruct(a.shape, a.dtype) for a in arrays),
@@ -462,7 +469,6 @@
             pltpu.VMEM((RATIO, TILES, 1, QUARTER), F32),
             pltpu.VMEM((RATIO, TILES, 1, QUARTER), F32),
             pltpu.VMEM((RATIO, 1, QUARTER), F32),
-            pltpu.VMEM((RATIO, HEAD_DIM, QUARTER), F32),
             pltpu.VMEM((QUARTER, HEAD_DIM), F32),
             pltpu.VMEM((QUARTER, HEAD_DIM), F32),
             pltpu.VMEM((RATIO, QUARTER, HEAD_DIM), BF16),

time: 49.4 us -> 49.3 us (level)
  no operation moved by 1% of the time
where the time goes in v1:
time: 49.3 us; the launch traced here: 49.1 us
  Pallas kernels  48.3 us (98%)
  between operations  0.8 us (2%)
    pallas_call x1, Pallas kernels, body(): pl.pallas_call(functools.partial(kernel, groups), out_shape=(jax.ShapeDty...  46.3 us
    pallas_call x1, Pallas kernels, copied(): pl.pallas_call(copy_kernel, out_shape=tuple((jax.ShapeDtypeStruct(a.shape...  2.01 us

profile of v1, /device:TPU:4, one launch (start us, length us, event | category | flops | bytes accessed | tf_op | source)
XLA Modules:
  0.0 49.1 jit_solution(2015292334276959694)
XLA Ops:
  0.6 46.3 %shard_map.76 = (bf16[128,2048]{1,0:T(8,128)(2,1)}, bf16[128,512]{1,0:T(8,128)(2,1)}, bf16[128,512]{1,0:T(8,128)(2,1)}) custom-call(bf16[128,2048]{1,0:T(8,128)(2,1)} %q_ref.1, bf16[128,2048]{1,0:T(8,128)(2,1)} %g_ref.1, bf16[128,512]{1,0:T(8,128)(2,1)} %k_ref.1, bf16[128,512]{1,0:T(8,128)(2,1)} %v_ref.1, s32[1,128]{1,0:T(1,128)} %bitcast.1), custom_call_target="tpu_custom_call" | custom-call | tf_op jit(solution)/shard_map/pallas_call | solution.py:450
  46.9 2.0 %shard_map.77 = (bf16[128,2048]{1,0:T(8,128)(2,1)}, bf16[128,512]{1,0:T(8,128)(2,1)}, bf16[128,512]{1,0:T(8,128)(2,1)}) custom-call(bf16[128,2048]{1,0:T(8,128)(2,1)} %get-tuple-element.6.refs_0_, bf16[128,512]{1,0:T(8,128)(2,1)} %get-tuple-element.7.refs_1_, bf16[128,512]{1,0:T(8,128)(2,1)} %get-tuple-element.8.refs_2_), custom_call_target="tpu_custom_call" | custom-call | tf_op jit(solution)/shard_map/pallas_call | solution.py:438
